TPU v7x, 32 devices: a whole 2x2x4 slice. The times are simulated.
32 devices in a mesh: traj: 2 (over x), frame: 4 (over y, core), patch: 4 (over z).
Axes of the slice: x: 2, y: 2, z: 4, core: 2. Of those that a mesh axis runs over, the one named last changes fastest.
Arguments:
- queries: float32 [16, 256, 1024], P(('traj', 'frame'), 'patch'), parts along dimension 0, may hold values from -64 to 64
- key_rows: float32 [16, 256, 1024], P(('traj', 'frame'), 'patch'), parts along dimension 0, may hold values from -5 to 5
- value_rows: float32 [16, 256, 1024], P(('traj', 'frame'), 'patch'), parts along dimension 0, may hold values from -6 to 6
- cotangent: float32 [16, 256, 1024], P(('traj', 'frame'), 'patch'), parts along dimension 0, may hold values from -6 to 6
- lookback: int32 [16], P(('traj', 'frame')), parts along dimension 0, may hold values from 2 to 6
- window: int32 [32, 12], P(('traj', 'patch')), parts along dimension 0, may hold values from 0 to 15, as said below
Outputs:
- mixed: float32 [16, 256, 1024], P(('traj', 'frame'), 'patch'), parts along dimension 0
- grad_queries: float32 [16, 256, 1024], P(('traj', 'frame'), 'patch'), parts along dimension 0
- grad_keys: float32 [16, 256, 1024], P(('traj', 'frame'), 'patch'), parts along dimension 0
- grad_values: float32 [16, 256, 1024], P(('traj', 'frame'), 'patch'), parts along dimension 0
There are 2 independent parts, one for each index of `traj`. A program takes and returns all parts, laid end to end along the dimension named above; each array names one. Nothing has to cross between parts.
Inputs may be any that keep to these rules, and one draw needn't show every extreme that they name: `window`: row b lists 12 distinct blocks: b itself first, then blocks at cyclic distance 1 to 6 from b among the 16 blocks.
All inputs are finite; a program needn't handle non-finite values.
Results may differ from a plain program's by a relative error of at most 0.0003.
Values sent between devices are 32-bit elements; how exact they have to be, the bound alone decides.
No kernel may reach another device: no remote copies, remote signals or barrier semaphores. Data moves between devices by JAX's collectives and lax.ppermute only.
A program may use at most 128 MiB of HBM per device.

v0:
```python
import math

import jax
import jax.numpy as jnp
from jax import lax
from jax.experimental import pallas as pl
from jax.experimental.pallas import tpu as pltpu
from jax.sharding import PartitionSpec as P

H = 16
BLK = 16
LOOK = 6
REACH = 6


def shifted(x, axis, by):
    count = lax.axis_size(axis)
    pairs = [(i, i + by) for i in range(count) if 0 <= i + by < count]
    return lax.ppermute(x, axis, pairs)


def passed_along(block, axis, distance):
    devices = range(lax.axis_size(axis))
    route = [((i - distance) % len(devices), i) for i in devices]
    return lax.ppermute(block, axis, route)


def split_heads(tensor, size_head):
    return tensor.reshape(tensor.shape[0], tensor.shape[1], H, size_head)


def shards_general(queries, key_rows, value_rows, cotangent, lookback, window):
    frames_here, patches_here, model_width = queries.shape
    size_head = model_width // H
    score_scale = 1.0 / math.sqrt(size_head)
    highest = lax.Precision.HIGHEST
    frame_index = lax.axis_index("frame")
    cycle_depth = (LOOK + frames_here - 2) // frames_here
    earlier = []
    carried = (key_rows, value_rows)
    for distance in range(cycle_depth):
        carried = shifted((carried[0], carried[1]), "frame", 1)
        earlier.append(carried)
    bank_keys = jnp.concatenate(
        [earlier[cycle_depth - 1 - number][0] for number in range(cycle_depth)] + [key_rows], axis=0
    )
    bank_values = jnp.concatenate(
        [earlier[cycle_depth - 1 - number][1] for number in range(cycle_depth)] + [value_rows],
        axis=0,
    )
    bank_frames = bank_keys.shape[0]
    q_heads = split_heads(queries, size_head)
    key_heads = split_heads(bank_keys, size_head)
    value_heads = split_heads(bank_values, size_head)
    query_frame = frame_index * frames_here + jnp.arange(frames_here, dtype=jnp.int32)
    key_frame = (frame_index - cycle_depth) * frames_here + jnp.arange(bank_frames, dtype=jnp.int32)
    offset = query_frame[:, None] - key_frame[None, :]
    visible = (offset >= 0) & (offset < lookback[:, None]) & (key_frame[None, :] >= 0)
    scores = jnp.einsum("fphe,jphe->phfj", q_heads, key_heads, precision=highest) * score_scale
    scores = jnp.where(visible, scores, -jnp.inf)
    weights = jax.nn.softmax(scores, axis=-1)
    temporal = jnp.einsum("phfj,jphe->fphe", weights, value_heads, precision=highest).reshape(
        frames_here, patches_here, model_width
    )
    patch_count = lax.axis_size("patch")
    patch_index = lax.axis_index("patch")
    blocks_here = patches_here // BLK
    reach_devices = -(-REACH // blocks_here)
    offsets = []
    for stride in range(-reach_devices, reach_devices + 1):
        if all(((stride - earlier_step) % patch_count != 0 for earlier_step in offsets)):
            offsets.append(stride)
    entries = []
    running_base = 0
    for stride in offsets:
        count_here = blocks_here if stride != 0 and abs(stride) == reach_devices else blocks_here
        first_block = 0 if stride >= 0 else blocks_here - count_here
        entries.append((stride, first_block, count_here, running_base))
        running_base = running_base + count_here
    count_slots = running_base
    near_banks = []
    for stride, first_block, count_here, base_slot in entries:
        rows_from = first_block * BLK
        rows_to = (first_block + count_here) * BLK
        piece = (key_rows, temporal)
        if stride == 0:
            near_banks.append(piece)
        else:
            near_banks.append(passed_along((piece[0], piece[1]), "patch", -stride))
    near_keys = jnp.concatenate([entry[0] for entry in near_banks], axis=1)
    near_values = jnp.concatenate([entry[1] for entry in near_banks], axis=1)
    owner_device = window // blocks_here
    relative = (owner_device - patch_index) % patch_count
    base_of = jnp.zeros(window.shape, jnp.int32)
    first_of = jnp.zeros(window.shape, jnp.int32)
    for stride, first_block, count_here, base_slot in entries:
        matches = relative == stride % patch_count
        base_of = jnp.where(matches, base_slot, base_of)
        first_of = jnp.where(matches, first_block, first_of)
    slot_index = base_of + window % blocks_here - first_of
    window_count = window.shape[1]
    key_blocks = near_keys.reshape(frames_here, count_slots, BLK, model_width)
    value_blocks = near_values.reshape(frames_here, count_slots, BLK, model_width)

    def frame_step(frame_items):
        query_part, key_part, value_part, grad_part = frame_items
        key_win = key_part[slot_index].reshape(blocks_here, window_count * BLK, H, size_head)
        value_win = value_part[slot_index].reshape(blocks_here, window_count * BLK, H, size_head)
        query_win = query_part.reshape(blocks_here, BLK, H, size_head)
        grad_win = grad_part.reshape(blocks_here, BLK, H, size_head)
        logits = jnp.einsum("bxhe,byhe->bhxy", query_win, key_win, precision=highest) * score_scale
        attention = jax.nn.softmax(logits, axis=-1)
        mixed_rows = jnp.einsum("bhxy,byhe->bxhe", attention, value_win, precision=highest)
        grad_attention = jnp.einsum("bxhe,byhe->bhxy", grad_win, value_win, precision=highest)
        grad_logits = attention * (
            grad_attention - jnp.sum(attention * grad_attention, axis=-1, keepdims=True)
        )
        grad_query = (
            jnp.einsum("bhxy,byhe->bxhe", grad_logits, key_win, precision=highest) * score_scale
        )
        grad_key = (
            jnp.einsum("bhxy,bxhe->byhe", grad_logits, query_win, precision=highest) * score_scale
        )
        grad_value = jnp.einsum("bhxy,bxhe->byhe", attention, grad_win, precision=highest)
        block_shape = (blocks_here, window_count, BLK, model_width)
        key_back = (
            jnp.zeros((count_slots, BLK, model_width), jnp.float32)
            .at[slot_index]
            .add(grad_key.reshape(block_shape))
        )
        value_back = (
            jnp.zeros((count_slots, BLK, model_width), jnp.float32)
            .at[slot_index]
            .add(grad_value.reshape(block_shape))
        )
        return (
            mixed_rows.reshape(patches_here, model_width),
            grad_query.reshape(patches_here, model_width),
            key_back,
            value_back,
        )

    mixed, grad_query_space, key_back, value_back = lax.map(
        frame_step, (queries, key_blocks, value_blocks, cotangent)
    )
    key_back = key_back.reshape(frames_here, count_slots * BLK, model_width)
    value_back = value_back.reshape(frames_here, count_slots * BLK, model_width)
    grad_key_space = jnp.zeros(queries.shape, jnp.float32)
    grad_temporal = jnp.zeros(queries.shape, jnp.float32)
    for stride, first_block, count_here, base_slot in entries:
        slot_from = base_slot * BLK
        slot_to = (base_slot + count_here) * BLK
        returned = (key_back[:, slot_from:slot_to], value_back[:, slot_from:slot_to])
        if stride != 0:
            returned = passed_along((returned[0], returned[1]), "patch", stride)
        rows_from = first_block * BLK
        rows_to = (first_block + count_here) * BLK
        grad_key_space = grad_key_space.at[:, rows_from:rows_to].add(returned[0])
        grad_temporal = grad_temporal.at[:, rows_from:rows_to].add(returned[1])
    grad_heads = split_heads(grad_temporal, size_head)
    grad_weights = jnp.einsum("fphe,jphe->phfj", grad_heads, value_heads, precision=highest)
    grad_scores = weights * (grad_weights - jnp.sum(weights * grad_weights, axis=-1, keepdims=True))
    grad_query_time = (
        jnp.einsum("phfj,jphe->fphe", grad_scores, key_heads, precision=highest) * score_scale
    )
    key_terms = (
        jnp.einsum("phfj,fphe->jphe", grad_scores, q_heads, precision=highest) * score_scale
    ).reshape(cycle_depth + 1, frames_here, patches_here, model_width)
    value_terms = jnp.einsum("phfj,fphe->jphe", weights, grad_heads, precision=highest).reshape(
        cycle_depth + 1, frames_here, patches_here, model_width
    )
    carried = (key_terms[0], value_terms[0])
    for distance in range(1, cycle_depth + 1):
        carried = shifted((carried[0], carried[1]), "frame", -1)
        carried = (carried[0] + key_terms[distance], carried[1] + value_terms[distance])
    grad_key_time, grad_value_time = carried
    grad_queries = grad_query_space + grad_query_time.reshape(
        frames_here, patches_here, model_width
    )
    grad_keys = grad_key_space + grad_key_time
    return (mixed, grad_queries, grad_keys, grad_value_time)


LANES = 128
INFO = 8


def swap_halves(x):
    return pltpu.roll(x, LANES // 2, x.ndim - 1)


def interleave(first, second):
    low = lax.broadcasted_iota(jnp.int32, first.shape, first.ndim - 1) < LANES // 2
    return (
        jnp.where(low, first, swap_halves(second)),
        jnp.where(low, swap_halves(first), second),
    )


def pack_kernel(window_ref, lookback_ref, *refs):
    arrays, out_ref = refs[:-1], refs[-1]
    rows = arrays[0].shape[1]
    row = lax.broadcasted_iota(jnp.int32, (INFO, LANES), 0)
    lane = lax.broadcasted_iota(jnp.int32, (INFO, LANES), 1)
    info = jnp.zeros((INFO, LANES), jnp.int32)
    for block in range(rows // BLK):
        for column in range(window_ref.shape[1]):
            at = block * BLK + (column // INFO) * (LANES // 2)
            here = (row == column % INFO) & (lane >= at) & (lane < at + BLK)
            info = jnp.where(here, window_ref[block, column], info)
    for frame in range(2):
        here = (row == INFO - 2 + frame) & (lane >= LANES // 2)
        info = jnp.where(here, lookback_ref[frame], info)
    info = info.astype(jnp.float32)
    for pair in range(H // 2):
        cols = slice(pair * LANES, (pair + 1) * LANES)
        for number, ref in enumerate(arrays):
            at = slice(number * rows, (number + 1) * rows)
            out_ref[2 * pair, at], out_ref[2 * pair + 1, at] = interleave(
                ref[0, :, cols], ref[1, :, cols]
            )
        at = slice(len(arrays) * rows, len(arrays) * rows + INFO)
        out_ref[2 * pair, at] = info
        out_ref[2 * pair + 1, at] = info


def unpack_kernel(in_ref, *out_refs):
    rows = out_refs[0].shape[1]
    for pair in range(H // 2):
        cols = slice(pair * LANES, (pair + 1) * LANES)
        for number, ref in enumerate(out_refs):
            at = slice(number * rows, (number + 1) * rows)
            ref[0, :, cols], ref[1, :, cols] = interleave(
                in_ref[2 * pair, at], in_ref[2 * pair + 1, at]
            )


def dot(a, b, dims):
    return lax.dot_general(
        a, b, (dims, ((), ())), precision=lax.Precision.HIGHEST, preferred_element_type=jnp.float32
    )


NN = ((1,), (0,))
NT = ((1,), (1,))


def head_kernel(
    frames, patches, columns, in_ref, out_ref, qt, kt, vt, ct, tt, tn, gt, gq, gk, gv, wts, bias
):
    rows = (in_ref.shape[1] - INFO) // 4
    size = LANES // 2
    pairs = frames // 2
    parts = patches // rows
    scale = 1.0 / math.sqrt(size)

    def natural(number, pair):
        at = pl.ds(number * rows, rows)
        return in_ref[pl.ds(pair * parts, parts), at].reshape(patches, LANES)

    info = [in_ref[part, 4 * rows : 4 * rows + INFO] for part in range(parts)]
    low = lax.broadcasted_iota(jnp.int32, (INFO, LANES), 1) < LANES // 2
    firsts, lasts = [], []
    for part in range(0, parts, 2):
        first, last = interleave(info[part], info[part + 1])
        firsts.append(first)
        lasts.append(last)
    first = jnp.concatenate(firsts, axis=1)
    last = jnp.concatenate(lasts, axis=1)
    key_block = (lax.broadcasted_iota(jnp.int32, (patches, patches), 0) // BLK).astype(jnp.float32)
    seen = key_block == first[0:1]
    for column in range(1, columns):
        of = first if column < INFO else last
        seen = seen | (key_block == of[column % INFO : column % INFO + 1])
    bias[...] = jnp.where(seen, 0.0, -jnp.inf)

    def turn(pair, carry):
        at = pl.ds(pair * LANES, LANES)
        qt[at] = natural(0, pair).T * scale
        kt[at] = natural(1, pair).T
        vt[at] = natural(2, pair).T
        ct[at] = natural(3, pair).T
        return carry

    lax.fori_loop(0, pairs, turn, 0)

    def frame_rows(ref, frame, cols):
        return ref[frame * size : (frame + 1) * size, cols]

    lookbacks = []
    for frame in range(frames):
        tile = in_ref[(frame // 2) * parts, 4 * rows : 4 * rows + INFO]
        _, tile = interleave(tile, tile)
        lookbacks.append(tile[INFO - 2 + frame % 2 : INFO - 1 + frame % 2])

    for chunk in range(patches // LANES):
        cols = slice(chunk * LANES, (chunk + 1) * LANES)
        for frame in range(frames):
            q = frame_rows(qt, frame, cols)
            keys = range(max(0, frame - LOOK + 1), frame + 1)
            scores = []
            for key in keys:
                score = jnp.sum(q * frame_rows(kt, key, cols), axis=0, keepdims=True)
                gap = float(frame - key)
                scores.append(jnp.where(lookbacks[frame] > gap, score, -jnp.inf))
            top = scores[0]
            for score in scores[1:]:
                top = jnp.maximum(top, score)
            exps = [jnp.exp(score - top) for score in scores]
            total = exps[0]
            for term in exps[1:]:
                total = total + term
            value = jnp.zeros((size, LANES), jnp.float32)
            for key, term in zip(keys, exps):
                weight = term / total
                wts[frame, frame - key : frame - key + 1, cols] = weight
                value = value + weight * frame_rows(vt, key, cols)
            tt[frame * size : (frame + 1) * size, cols] = value

    def spatial(pair, carry):
        at = pl.ds(pair * LANES, LANES)
        tn[...] = tt[at].T
        keys = natural(1, pair)
        zeros = jnp.zeros((size, patches), jnp.float32)
        mixed = []
        for half in range(2):
            mine = pl.ds(pair * LANES + half * size, size)

            def padded(x):
                return jnp.concatenate([x, zeros] if half == 0 else [zeros, x], axis=0)

            logits = dot(keys, padded(qt[mine]), NN) + bias[...]
            top = jnp.max(logits, axis=0, keepdims=True)
            weights = jnp.exp(logits - top)
            weights = weights / jnp.sum(weights, axis=0, keepdims=True)
            mix = dot(tt[mine], weights, NN)
            mixed.append(mix)
            grad = ct[mine]
            delta = jnp.sum(grad * mix, axis=0, keepdims=True)
            grad_logits = weights * (dot(tn[...], padded(grad), NN) - delta)
            gq[mine] = dot(kt[mine], grad_logits, NN)
            gk[mine] = dot(qt[mine], grad_logits, NT)
            gt[mine] = dot(grad, weights, NT)
        mixed = jnp.concatenate(mixed, axis=0).T.reshape(parts, rows, LANES)
        out_ref[pl.ds(pair * parts, parts), pl.ds(0, rows)] = mixed
        return carry

    lax.fori_loop(0, pairs, spatial, 0)

    gv[...] = jnp.zeros(gv.shape, jnp.float32)
    for chunk in range(patches // LANES):
        cols = slice(chunk * LANES, (chunk + 1) * LANES)
        for frame in range(frames):
            mine = slice(frame * size, (frame + 1) * size)
            q = frame_rows(qt, frame, cols)
            grad = frame_rows(gt, frame, cols)
            keys = range(max(0, frame - LOOK + 1), frame + 1)
            weights, grads = [], []
            inner = jnp.zeros((1, LANES), jnp.float32)
            for key in keys:
                weight = wts[frame, frame - key : frame - key + 1, cols]
                term = jnp.sum(grad * frame_rows(vt, key, cols), axis=0, keepdims=True)
                inner = inner + weight * term
                weights.append(weight)
                grads.append(term)
            grad_q = gq[mine, cols]
            for key, weight, term in zip(keys, weights, grads):
                of = slice(key * size, (key + 1) * size)
                score = weight * (term - inner)
                grad_q = grad_q + score * kt[of, cols]
                gk[of, cols] = gk[of, cols] + score * q
                gv[of, cols] = gv[of, cols] + weight * grad
            gq[mine, cols] = grad_q * scale

    def turn_back(pair, carry):
        at = pl.ds(pair * LANES, LANES)
        for number, ref in ((1, gq), (2, gk), (3, gv)):
            out_ref[pl.ds(pair * parts, parts), pl.ds(number * rows, rows)] = (
                ref[at].T.reshape(parts, rows, LANES)
            )
        return carry

    lax.fori_loop(0, pairs, turn_back, 0)


def shards_by_head(queries, key_rows, value_rows, cotangent, lookback, window):
    frames_here, patches_here, model_width = queries.shape
    group = ("frame", "patch")
    frames = frames_here * lax.axis_size("frame")
    patches = patches_here * lax.axis_size("patch")
    vmem = pl.BlockSpec(memory_space=pltpu.VMEM)
    smem = pl.BlockSpec(memory_space=pltpu.SMEM)
    params = pltpu.CompilerParams(vmem_limit_bytes=40 * 1024 * 1024)
    packed = pl.pallas_call(
        pack_kernel,
        out_shape=jax.ShapeDtypeStruct((H, 4 * patches_here + INFO, LANES), jnp.float32),
        in_specs=[smem, smem] + [vmem] * 4,
        out_specs=vmem,
        compiler_params=params,
        name="pack_heads",
    )(window, lookback, queries, key_rows, value_rows, cotangent)
    by_head = lax.all_to_all(packed, group, 0, 0, tiled=True)
    whole = pltpu.VMEM((frames * LANES // 2, patches), jnp.float32)
    done = pl.pallas_call(
        lambda *refs: head_kernel(frames, patches, window.shape[1], *refs),
        out_shape=jax.ShapeDtypeStruct((H, 4 * patches_here, LANES), jnp.float32),
        in_specs=[vmem],
        out_specs=vmem,
        scratch_shapes=[whole] * 5
        + [pltpu.VMEM((patches, LANES), jnp.float32)]
        + [whole] * 4
        + [pltpu.VMEM((frames, 8, patches), jnp.float32)]
        + [pltpu.VMEM((patches, patches), jnp.float32)],
        compiler_params=params,
        name="one_head",
    )(by_head)
    by_rows = lax.all_to_all(done, group, 0, 0, tiled=True)
    return pl.pallas_call(
        unpack_kernel,
        out_shape=[jax.ShapeDtypeStruct(queries.shape, jnp.float32)] * 4,
        in_specs=[vmem],
        out_specs=[vmem] * 4,
        compiler_params=params,
        name="unpack_heads",
    )(by_rows)


def shards(queries, key_rows, value_rows, cotangent, lookback, window):
    frames_here, patches_here, model_width = queries.shape
    fits = (
        lax.axis_size("frame") * lax.axis_size("patch") == H
        and frames_here == 2
        and patches_here == LANES // 2
        and lax.axis_size("patch") % 2 == 0
        and model_width == H * (LANES // 2)
    )
    form = shards_by_head if fits else shards_general
    return tuple(form(queries, key_rows, value_rows, cotangent, lookback, window))


def solution(mesh):
    in_specs = (
        P(("traj", "frame"), "patch", None),
        P(("traj", "frame"), "patch", None),
        P(("traj", "frame"), "patch", None),
        P(("traj", "frame"), "patch", None),
        P(("traj", "frame")),
        P(("traj", "patch"), None),
    )
    out_specs = (
        P(("traj", "frame"), "patch", None),
        P(("traj", "frame"), "patch", None),
        P(("traj", "frame"), "patch", None),
        P(("traj", "frame"), "patch", None),
    )
    return jax.shard_map(shards, mesh=mesh, in_specs=in_specs, out_specs=out_specs, check_vma=False)
```

profile of v0, /device:TPU:0, one launch (start us, length us, event | category | flops | bytes accessed | tf_op | source)
XLA Modules:
  0.0 138.4 jit_solution(8936223459652304429)
XLA Ops:
  0.6 0.0 copy-start
  0.6 1.0 copy-done
  1.7 0.0 copy-start.1
  1.7 1.0 copy-done.1
  2.7 0.0 copy-start.2
  2.7 1.0 copy-done.2
  3.8 0.0 copy-start.3
  3.8 1.0 copy-done.3
  4.8 0.0 copy-start.4
  4.8 0.7 copy-done.4
  5.5 0.0 copy-start.5
  5.5 0.7 copy-done.5
  6.1 1.2 pack_heads.1
  7.3 58.2 %all_to_all.10.refs_0_ = f32[16,264,128]{2,1,0:T(8,128)S(1)} all-to-all(f32[16,264,128]{2,1,0:T(8,128)S(1)} %pack_heads.1), channel_id=1, replica_groups=mesh['traj'=2,'frame'=4,'patch'=4] {'frame','patch'}, dimensions={0} | all-to-all | bytes 4325376 | tf_op jit(solution)/shard_map/all_to_all | solution.py:402
  65.6 18.6 %one_head.1 = f32[16,256,128]{2,1,0:T(8,128)S(1)} custom-call(f32[16,264,128]{2,1,0:T(8,128)S(1)} %all_to_all.10.refs_0_), custom_call_target="tpu_custom_call" | custom-call | tf_op jit(solution)/shard_map/one_head/pallas_call | solution.py:404
  84.2 52.4 %all_to_all.11.in_ref = f32[16,256,128]{2,1,0:T(8,128)S(1)} all-to-all(f32[16,256,128]{2,1,0:T(8,128)S(1)} %one_head.1), channel_id=1, replica_groups=mesh['traj'=2,'frame'=4,'patch'=4] {'frame','patch'}, dimensions={0} | all-to-all | bytes 4194304 | tf_op jit(solution)/shard_map/all_to_all | solution.py:417
  136.6 1.9 %unpack_heads.1 = (f32[2,64,1024]{2,1,0:T(8,128)}, f32[2,64,1024]{2,1,0:T(8,128)}, f32[2,64,1024]{2,1,0:T(8,128)}, f32[2,64,1024]{2,1,0:T(8,128)}) custom-call(f32[16,256,128]{2,1,0:T(8,128)S(1)} %all_to_all.11.in_ref), custom_call_target="tpu_custom_call" | custom-call | tf_op jit(solution)/shard_map/unpack_heads/pallas_call | solution.py:418
Async XLA Ops:
  0.6 1.0 copy-start
  1.7 1.0 copy-start.1
  2.7 1.0 copy-start.2
  3.8 1.0 copy-start.3
  4.8 0.7 copy-start.4
  5.5 0.7 copy-start.5
where the time goes:
time: 139 us; the launch traced here: 138 us
  blocking collectives  111 us (80%)
  Pallas kernels  21.6 us (16%)
  local copies, waits for them, and re-layouts  5.49 us (4%)
    all_to_all x1, blocking collectives, shards_by_head(): by_head = lax.all_to_all(packed, group, 0, 0, tiled=True)  58.2 us
    all_to_all x1, blocking collectives, shards_by_head(): by_rows = lax.all_to_all(done, group, 0, 0, tiled=True)  52.4 us
    pallas_call x1, Pallas kernels, shards_by_head(): pl.pallas_call(lambda *refs: head_kernel(frames, patches, window.shape[1]...  18.6 us
    unnamed x12, local copies, waits for them, and re-layouts  5.49 us

commit v1 on v0

--- a/solution.py
+++ b/solution.py
@@ -236,9 +236,24 @@
 
 
 def dot(a, b, dims):
-    return lax.dot_general(
-        a, b, (dims, ((), ())), precision=lax.Precision.HIGHEST, preferred_element_type=jnp.float32
-    )
+    return lax.dot_general(a, b, (dims, ((), ())), preferred_element_type=jnp.float32)
+
+
+def split(x):
+    high = x.astype(jnp.bfloat16)
+    return high, (x - high.astype(jnp.float32)).astype(jnp.bfloat16)
+
+
+def stacked(x, times):
+    high, low = split(x)
+    return jnp.concatenate([high] * times + [low] * times, axis=0)
+
+
+def heads_dot(x, high, low, dims):
+    both = stacked(x, 1)
+    size = x.shape[0]
+    out = dot(both, high, dims)
+    return out[:size] + (out[size:] + dot(both[:size], low, dims))
 
 
 NN = ((1,), (0,))
@@ -246,7 +261,7 @@
 
 
 def head_kernel(
-    frames, patches, columns, in_ref, out_ref, qt, kt, vt, ct, tt, tn, gt, gq, gk, gv, wts, bias
+    frames, patches, columns, in_ref, out_ref, qt, kt, vt, ct, tt, gt, gq, gk, gv, wts, bias
 ):
     rows = (in_ref.shape[1] - INFO) // 4
     size = LANES // 2
@@ -282,7 +297,12 @@
         ct[at] = natural(3, pair).T
         return carry
 
-    lax.fori_loop(0, pairs, turn, 0)
+    lax.fori_loop(0, pairs, turn, 0, unroll=True)
+
+    def halves(x):
+        high = x.astype(jnp.bfloat16).astype(jnp.float32)
+        sides = interleave(high, x - high)
+        return [jnp.concatenate([side.astype(jnp.bfloat16)] * 2, axis=1) for side in sides]
 
     def frame_rows(ref, frame, cols):
         return ref[frame * size : (frame + 1) * size, cols]
@@ -319,33 +339,30 @@
 
     def spatial(pair, carry):
         at = pl.ds(pair * LANES, LANES)
-        tn[...] = tt[at].T
-        keys = natural(1, pair)
-        zeros = jnp.zeros((size, patches), jnp.float32)
+        keys = halves(natural(1, pair))
+        values = halves(tt[at].T)
         mixed = []
         for half in range(2):
             mine = pl.ds(pair * LANES + half * size, size)
-
-            def padded(x):
-                return jnp.concatenate([x, zeros] if half == 0 else [zeros, x], axis=0)
-
-            logits = dot(keys, padded(qt[mine]), NN) + bias[...]
+            query, grad = qt[mine], ct[mine]
+            logits = dot(keys[half], stacked(query, 2), NN) + bias[...]
+            grad_weights = dot(values[half], stacked(grad, 2), NN)
             top = jnp.max(logits, axis=0, keepdims=True)
-            weights = jnp.exp(logits - top)
-            weights = weights / jnp.sum(weights, axis=0, keepdims=True)
-            mix = dot(tt[mine], weights, NN)
+            exps = jnp.exp(logits - top)
+            share = 1.0 / jnp.sum(exps, axis=0, keepdims=True)
+            high, low = split(exps)
+            mix = heads_dot(tt[mine], high, low, NN) * share
             mixed.append(mix)
-            grad = ct[mine]
+            gt[mine] = heads_dot(grad * share, high, low, NT)
             delta = jnp.sum(grad * mix, axis=0, keepdims=True)
-            grad_logits = weights * (dot(tn[...], padded(grad), NN) - delta)
-            gq[mine] = dot(kt[mine], grad_logits, NN)
-            gk[mine] = dot(qt[mine], grad_logits, NT)
-            gt[mine] = dot(grad, weights, NT)
+            high, low = split(exps * (grad_weights - delta))
+            gq[mine] = heads_dot(kt[mine], high, low, NN) * share
+            gk[mine] = heads_dot(query * share, high, low, NT)
         mixed = jnp.concatenate(mixed, axis=0).T.reshape(parts, rows, LANES)
         out_ref[pl.ds(pair * parts, parts), pl.ds(0, rows)] = mixed
         return carry
 
-    lax.fori_loop(0, pairs, spatial, 0)
+    lax.fori_loop(0, pairs, spatial, 0, unroll=True)
 
     gv[...] = jnp.zeros(gv.shape, jnp.float32)
     for chunk in range(patches // LANES):
@@ -380,7 +397,7 @@
             )
         return carry
 
-    lax.fori_loop(0, pairs, turn_back, 0)
+    lax.fori_loop(0, pairs, turn_back, 0, unroll=True)
 
 
 def shards_by_head(queries, key_rows, value_rows, cotangent, lookback, window):
@@ -406,9 +423,7 @@
         out_shape=jax.ShapeDtypeStruct((H, 4 * patches_here, LANES), jnp.float32),
         in_specs=[vmem],
         out_specs=vmem,
-        scratch_shapes=[whole] * 5
-        + [pltpu.VMEM((patches, LANES), jnp.float32)]
-        + [whole] * 4
+        scratch_shapes=[whole] * 9
         + [pltpu.VMEM((frames, 8, patches), jnp.float32)]
         + [pltpu.VMEM((patches, patches), jnp.float32)],
         compiler_params=params,

time: 139 us -> 126 us (0.906)
  Pallas kernels: 21.6 us -> 8.47 us
    pallas_call x1, Pallas kernels: 18.6 us -> 5.43 us  [shards_by_head(): pl.pallas_call(lambda *refs: head_kernel(frames, patches, window.shape[1]...]
where the time goes in v1:
time: 126 us; the launch traced here: 125 us
  blocking collectives  111 us (88%)
  Pallas kernels  8.47 us (7%)
  local copies, waits for them, and re-layouts  5.49 us (4%)
    all_to_all x1, blocking collectives, shards_by_head(): by_head = lax.all_to_all(packed, group, 0, 0, tiled=True)  58.2 us
    all_to_all x1, blocking collectives, shards_by_head(): by_rows = lax.all_to_all(done, group, 0, 0, tiled=True)  52.4 us
    unnamed x12, local copies, waits for them, and re-layouts  5.49 us
    pallas_call x1, Pallas kernels, shards_by_head(): pl.pallas_call(lambda *refs: head_kernel(frames, patches, window.shape[1]...  5.43 us

profile of v1, /device:TPU:0, one launch (start us, length us, event | category | flops | bytes accessed | tf_op | source)
XLA Modules:
  0.0 125.3 jit_solution(13704728255195313956)
XLA Ops:
  0.6 0.0 copy-start
  0.6 1.0 copy-done
  1.7 0.0 copy-start.1
  1.7 1.0 copy-done.1
  2.7 0.0 copy-start.2
  2.7 1.0 copy-done.2
  3.8 0.0 copy-start.3
  3.8 1.0 copy-done.3
  4.8 0.0 copy-start.4
  4.8 0.7 copy-done.4
  5.5 0.0 copy-start.5
  5.5 0.7 copy-done.5
  6.1 1.2 pack_heads.1
  7.3 58.2 %all_to_all.10.refs_0_ = f32[16,264,128]{2,1,0:T(8,128)S(1)} all-to-all(f32[16,264,128]{2,1,0:T(8,128)S(1)} %pack_heads.1), channel_id=1, replica_groups=mesh['traj'=2,'frame'=4,'patch'=4] {'frame','patch'}, dimensions={0} | all-to-all | bytes 4325376 | tf_op jit(solution)/shard_map/all_to_all | solution.py:419
  65.6 5.4 %one_head.1 = f32[16,256,128]{2,1,0:T(8,128)S(1)} custom-call(f32[16,264,128]{2,1,0:T(8,128)S(1)} %all_to_all.10.refs_0_), custom_call_target="tpu_custom_call" | custom-call | tf_op jit(solution)/shard_map/one_head/pallas_call | solution.py:421
  71.0 52.4 %all_to_all.11.in_ref = f32[16,256,128]{2,1,0:T(8,128)S(1)} all-to-all(f32[16,256,128]{2,1,0:T(8,128)S(1)} %one_head.1), channel_id=1, replica_groups=mesh['traj'=2,'frame'=4,'patch'=4] {'frame','patch'}, dimensions={0} | all-to-all | bytes 4194304 | tf_op jit(solution)/shard_map/all_to_all | solution.py:432
  123.4 1.9 %unpack_heads.1 = (f32[2,64,1024]{2,1,0:T(8,128)}, f32[2,64,1024]{2,1,0:T(8,128)}, f32[2,64,1024]{2,1,0:T(8,128)}, f32[2,64,1024]{2,1,0:T(8,128)}) custom-call(f32[16,256,128]{2,1,0:T(8,128)S(1)} %all_to_all.11.in_ref), custom_call_target="tpu_custom_call" | custom-call | tf_op jit(solution)/shard_map/unpack_heads/pallas_call | solution.py:433
Async XLA Ops:
  0.6 1.0 copy-start
  1.7 1.0 copy-start.1
  2.7 1.0 copy-start.2
  3.8 1.0 copy-start.3
  4.8 0.7 copy-start.4
  5.5 0.7 copy-start.5
